TPU v7x, 256 devices: a whole 4x4x8 slice. The times are simulated.
256 devices in a mesh: row: 8 (over x, core), col: 32 (over y, z).
Axes of the slice: x: 4, y: 4, z: 8, core: 2. Of those that a mesh axis runs over, the one named last changes fastest.
Arguments:
- features: bfloat16 [65536, 512], P('col', 'row'), may hold values from -6 to 6
- weight: bfloat16 [512, 512], replicated, may hold values from -0.25 to 0.25
- bias: float32 [512], replicated, may hold values from -3 to 3
- edge_src: int32 [512, 16384], P('row', 'col'), may hold values from 0 to 2047
- edge_dst: int32 [512, 16384], P('row', 'col'), may hold values from 0 to 127
- tile_count: int32 [512, 32], P('row', 'col'), may hold values from 0 to 512, as said below
Outputs:
- layer_out: bfloat16 [65536, 512], P(('row', 'col'))
Inputs may be any that keep to these rules, and one draw needn't show every extreme that they name: `tile_count`: entries of a tile past its count are padding and carry no edge. Some tile holds exactly 512 live edges from one sending block in every draw.
All inputs are finite; a program needn't handle non-finite values.
Results may differ from a plain program's by a relative error of at most 0.0034.
Values may be sent and summed in bfloat16 or wider, within the bound.
A program may use at most 128 MiB of HBM per device.

v0:
```python
import math

import jax
import jax.numpy as jnp
from jax import lax
from jax.sharding import PartitionSpec as P

TILE = 128


def live_mask_of(counts, slot_cap):
    slot_index = lax.broadcasted_iota(jnp.int32, (counts.shape[0], slot_cap), 1)
    return (slot_index < counts).astype(jnp.float32)


def tile_sums(source, target, weights, table):
    picked = jnp.take(table, source.reshape(-1), axis=0)
    picked = picked.reshape(source.shape[0], source.shape[1], table.shape[1])
    places = lax.broadcasted_iota(jnp.int32, (1, TILE, 1), 1)
    onehot = ((target[:, None, :] == places) * weights[:, None, :]).astype(jnp.bfloat16)
    sums = jnp.einsum("gts,gsf->gtf", onehot, picked, preferred_element_type=jnp.float32)
    counts = jnp.sum(onehot, axis=2, dtype=jnp.float32)
    return (sums, counts)


def source_counts(edge_src, live_mask, source_rows):
    tiles_dev, slot_cap = edge_src.shape
    group_size = math.gcd(tiles_dev, 4)
    group_shape = (tiles_dev // group_size, group_size * slot_cap)
    node_ids = lax.broadcasted_iota(jnp.int32, (1, source_rows), 1)

    def group_count(packed):
        sources, weights = packed
        onehot = (sources[:, None] == node_ids).astype(jnp.bfloat16)
        return jnp.dot(
            weights[None, :].astype(jnp.bfloat16), onehot, preferred_element_type=jnp.float32
        )[0]

    partial_counts = lax.map(
        group_count, (edge_src.reshape(group_shape), live_mask.reshape(group_shape))
    )
    return jnp.sum(partial_counts, axis=0)


def body(features, weight, bias, edge_src, edge_dst, tile_count):
    tiles_dev, slot_cap = edge_src.shape
    source_rows = features.shape[0]
    live_mask = live_mask_of(tile_count, slot_cap)
    out_local = source_counts(edge_src, live_mask, source_rows)
    out_degree = lax.psum(out_local, "row")
    scaled = (features.astype(jnp.float32) * lax.rsqrt(1.0 + out_degree)[:, None]).astype(
        jnp.bfloat16
    )
    panel_rows = lax.all_gather(scaled, "row", axis=1, tiled=True)
    group_size = math.gcd(tiles_dev, 4)

    def group_step(packed):
        return tile_sums(packed[0], packed[1], packed[2], panel_rows)

    group_shape = (tiles_dev // group_size, group_size, slot_cap)
    partial_rows, in_local = lax.map(
        group_step,
        (
            edge_src.reshape(group_shape),
            edge_dst.reshape(group_shape),
            live_mask.reshape(group_shape),
        ),
    )
    partial_rows = partial_rows.reshape(tiles_dev * TILE, panel_rows.shape[1])
    in_local = in_local.reshape(tiles_dev * TILE)
    aggregate, in_degree = (
        lax.psum_scatter(partial_rows, "col", scatter_dimension=0, tiled=True),
        lax.psum_scatter(in_local, "col", scatter_dimension=0, tiled=True),
    )
    normed = (aggregate * lax.rsqrt(1.0 + in_degree)[:, None]).astype(jnp.bfloat16)
    projected = jnp.dot(normed, weight, preferred_element_type=jnp.float32) + bias
    return jax.nn.relu(projected).astype(jnp.bfloat16)


def solution(mesh):
    in_specs = (P("col", "row"), P(), P(), P("row", "col"), P("row", "col"), P("row", "col"))
    out_specs = P(("row", "col"), None)
    return jax.shard_map(body, mesh=mesh, in_specs=in_specs, out_specs=out_specs, check_vma=False)
```

profile of v0, /device:TPU:8, one launch (start us, length us, event | category | flops | bytes accessed | tf_op | source)
XLA Modules:
  0.0 563.9 jit_solution(15547458476184358437)
XLA Ops:
  9.7 51.2 %while.24 = (s32[]{:T(128)}, f32[16,2048]{1,0:T(8,128)S(1)}, bf16[16,2048]{1,0:T(8,128)(2,1)S(1)}, s32[16,2048]{1,0:T(8,128)S(1)}, s32[]{:T(128)}, /*index=5*/s32[]{:T(128)}) while((s32[]{:T(128)}, f32[16,2048]{1,0:T(8,128)S(1)}, bf16[16,2048]{1,0:T(8,128)(2,1)S(1)}, s32[16,2048]{1,0:T(8,128)S(1)}, s32[]{:T(128)}, ...), condition=%wide.region_1.2_spmd.clone, body=%wide.region_0.1_spmd.clone.sunk | while | flops 12582914 | bytes 57425 | solution.py:39
  60.9 14.9 %psum.7 = f32[2048]{0:T(1024)S(1)} all-reduce(f32[2048]{0:T(1024)S(1)} %reduce_sum.18), channel_id=1, replica_groups=mesh['row'=8,'col'=32] {'row'}, use_global_device_ids=true, to_apply=%region_3.4 | all-reduce | flops 2048 | bytes 16384 | tf_op jit(solution)/shard_map/psum | solution.py:50
  76.9 28.0 %all-gather.2.cloned.1.call-done = bf16[2048,512]{0,1:T(8,128)(2,1)} async-done(((bf16[2048,64]{0,1:T(8,128)(2,1)}), bf16[2048,512]{0,1:T(8,128)(2,1)}) %all-gather.2.cloned.1.call-update) | async-done | bytes 2097168 | tf_op jit(solution)/shard_map/all_gather | solution.py:54
  107.7 201.8 %while.23 = (s32[]{:T(128)}, f32[16,4,128,512]{3,2,1,0:T(8,128)}, f32[16,4,128]{2,1,0:T(4,128)S(1)}, s32[16,4,512]{2,1,0:T(4,128)S(1)}, bf16[16,4,512]{2,1,0:T(4...) while((s32[]{:T(128)}, f32[16,4,128,512]{3,2,1,0:T(8,128)}, ...), condition=%wide.region_6.7_spmd, body=%wide.region_4.6_spmd.sunk | while | flops 271076864 | bytes 7481961 | solution.py:61
  107.8 9.2 %gather_fusion = bf16[2048,512]{1,0:T(8,128)(2,1)} fusion(bf16[2048,512]{1,0:T(8,128)(2,1)S(1)} %get-tuple-element.220, s32[2048]{0:T(1024)S(1)} %broadcast_clamp_fusion.2), kind=kCustom, calls=%fused_computation.clone.1 | custom fusion | bytes 4202496 | tf_op jit(solution)/shard_map/while/body/eval_jaxpr/jit(_take)/gather | solution.py:17
  120.4 9.2 %gather_fusion = bf16[2048,512]{1,0:T(8,128)(2,1)} fusion(bf16[2048,512]{1,0:T(8,128)(2,1)S(1)} %get-tuple-element.220, s32[2048]{0:T(1024)S(1)} %broadcast_clamp_fusion.2), kind=kCustom, calls=%fused_computation.clone.1 | custom fusion | bytes 4202496 | tf_op jit(solution)/shard_map/while/body/eval_jaxpr/jit(_take)/gather | solution.py:17
  133.1 9.2 %gather_fusion = bf16[2048,512]{1,0:T(8,128)(2,1)} fusion(bf16[2048,512]{1,0:T(8,128)(2,1)S(1)} %get-tuple-element.220, s32[2048]{0:T(1024)S(1)} %broadcast_clamp_fusion.2), kind=kCustom, calls=%fused_computation.clone.1 | custom fusion | bytes 4202496 | tf_op jit(solution)/shard_map/while/body/eval_jaxpr/jit(_take)/gather | solution.py:17
  145.7 9.2 %gather_fusion = bf16[2048,512]{1,0:T(8,128)(2,1)} fusion(bf16[2048,512]{1,0:T(8,128)(2,1)S(1)} %get-tuple-element.220, s32[2048]{0:T(1024)S(1)} %broadcast_clamp_fusion.2), kind=kCustom, calls=%fused_computation.clone.1 | custom fusion | bytes 4202496 | tf_op jit(solution)/shard_map/while/body/eval_jaxpr/jit(_take)/gather | solution.py:17
  158.3 9.2 %gather_fusion = bf16[2048,512]{1,0:T(8,128)(2,1)} fusion(bf16[2048,512]{1,0:T(8,128)(2,1)S(1)} %get-tuple-element.220, s32[2048]{0:T(1024)S(1)} %broadcast_clamp_fusion.2), kind=kCustom, calls=%fused_computation.clone.1 | custom fusion | bytes 4202496 | tf_op jit(solution)/shard_map/while/body/eval_jaxpr/jit(_take)/gather | solution.py:17
  170.8 9.2 %gather_fusion = bf16[2048,512]{1,0:T(8,128)(2,1)} fusion(bf16[2048,512]{1,0:T(8,128)(2,1)S(1)} %get-tuple-element.220, s32[2048]{0:T(1024)S(1)} %broadcast_clamp_fusion.2), kind=kCustom, calls=%fused_computation.clone.1 | custom fusion | bytes 4202496 | tf_op jit(solution)/shard_map/while/body/eval_jaxpr/jit(_take)/gather | solution.py:17
  183.5 9.2 %gather_fusion = bf16[2048,512]{1,0:T(8,128)(2,1)} fusion(bf16[2048,512]{1,0:T(8,128)(2,1)S(1)} %get-tuple-element.220, s32[2048]{0:T(1024)S(1)} %broadcast_clamp_fusion.2), kind=kCustom, calls=%fused_computation.clone.1 | custom fusion | bytes 4202496 | tf_op jit(solution)/shard_map/while/body/eval_jaxpr/jit(_take)/gather | solution.py:17
  196.1 9.2 %gather_fusion = bf16[2048,512]{1,0:T(8,128)(2,1)} fusion(bf16[2048,512]{1,0:T(8,128)(2,1)S(1)} %get-tuple-element.220, s32[2048]{0:T(1024)S(1)} %broadcast_clamp_fusion.2), kind=kCustom, calls=%fused_computation.clone.1 | custom fusion | bytes 4202496 | tf_op jit(solution)/shard_map/while/body/eval_jaxpr/jit(_take)/gather | solution.py:17
  208.7 9.2 %gather_fusion = bf16[2048,512]{1,0:T(8,128)(2,1)} fusion(bf16[2048,512]{1,0:T(8,128)(2,1)S(1)} %get-tuple-element.220, s32[2048]{0:T(1024)S(1)} %broadcast_clamp_fusion.2), kind=kCustom, calls=%fused_computation.clone.1 | custom fusion | bytes 4202496 | tf_op jit(solution)/shard_map/while/body/eval_jaxpr/jit(_take)/gather | solution.py:17
  217.9 3.2 fusion.34
  221.4 9.2 %gather_fusion = bf16[2048,512]{1,0:T(8,128)(2,1)} fusion(bf16[2048,512]{1,0:T(8,128)(2,1)S(1)} %get-tuple-element.220, s32[2048]{0:T(1024)S(1)} %broadcast_clamp_fusion.2), kind=kCustom, calls=%fused_computation.clone.1 | custom fusion | bytes 4202496 | tf_op jit(solution)/shard_map/while/body/eval_jaxpr/jit(_take)/gather | solution.py:17
  234.0 9.2 %gather_fusion = bf16[2048,512]{1,0:T(8,128)(2,1)} fusion(bf16[2048,512]{1,0:T(8,128)(2,1)S(1)} %get-tuple-element.220, s32[2048]{0:T(1024)S(1)} %broadcast_clamp_fusion.2), kind=kCustom, calls=%fused_computation.clone.1 | custom fusion | bytes 4202496 | tf_op jit(solution)/shard_map/while/body/eval_jaxpr/jit(_take)/gather | solution.py:17
  246.5 9.2 %gather_fusion = bf16[2048,512]{1,0:T(8,128)(2,1)} fusion(bf16[2048,512]{1,0:T(8,128)(2,1)S(1)} %get-tuple-element.220, s32[2048]{0:T(1024)S(1)} %broadcast_clamp_fusion.2), kind=kCustom, calls=%fused_computation.clone.1 | custom fusion | bytes 4202496 | tf_op jit(solution)/shard_map/while/body/eval_jaxpr/jit(_take)/gather | solution.py:17
  259.1 9.2 %gather_fusion = bf16[2048,512]{1,0:T(8,128)(2,1)} fusion(bf16[2048,512]{1,0:T(8,128)(2,1)S(1)} %get-tuple-element.220, s32[2048]{0:T(1024)S(1)} %broadcast_clamp_fusion.2), kind=kCustom, calls=%fused_computation.clone.1 | custom fusion | bytes 4202496 | tf_op jit(solution)/shard_map/while/body/eval_jaxpr/jit(_take)/gather | solution.py:17
  268.3 3.2 fusion.34
  271.8 9.2 %gather_fusion = bf16[2048,512]{1,0:T(8,128)(2,1)} fusion(bf16[2048,512]{1,0:T(8,128)(2,1)S(1)} %get-tuple-element.220, s32[2048]{0:T(1024)S(1)} %broadcast_clamp_fusion.2), kind=kCustom, calls=%fused_computation.clone.1 | custom fusion | bytes 4202496 | tf_op jit(solution)/shard_map/while/body/eval_jaxpr/jit(_take)/gather | solution.py:17
  284.4 9.2 %gather_fusion = bf16[2048,512]{1,0:T(8,128)(2,1)} fusion(bf16[2048,512]{1,0:T(8,128)(2,1)S(1)} %get-tuple-element.220, s32[2048]{0:T(1024)S(1)} %broadcast_clamp_fusion.2), kind=kCustom, calls=%fused_computation.clone.1 | custom fusion | bytes 4202496 | tf_op jit(solution)/shard_map/while/body/eval_jaxpr/jit(_take)/gather | solution.py:17
  297.0 9.2 %gather_fusion = bf16[2048,512]{1,0:T(8,128)(2,1)} fusion(bf16[2048,512]{1,0:T(8,128)(2,1)S(1)} %get-tuple-element.220, s32[2048]{0:T(1024)S(1)} %broadcast_clamp_fusion.2), kind=kCustom, calls=%fused_computation.clone.1 | custom fusion | bytes 4202496 | tf_op jit(solution)/shard_map/while/body/eval_jaxpr/jit(_take)/gather | solution.py:17
  311.4 131.8 %all-reduce = f32[8192]{0:T(1024)S(1)} all-reduce(f32[8192]{0:T(1024)S(1)} %bitcast.65), channel_id=3, replica_groups=mesh['row'=8,'col'=32] {'col'}, use_global_device_ids=true, to_apply=%region_8.9.clone | all-reduce | flops 8192 | bytes 65536
  443.3 111.7 %reduce-scatter.2.cloned.1.call-done = f32[256,512]{1,0:T(8,128)} async-done(((f32[8192,512]{1,0:T(8,128)}), f32[256,512]{1,0:T(8,128)}) %reduce-scatter.2.cloned.1.call-update) | async-done | bytes 524304 | tf_op jit(solution)/shard_map/reduce_scatter | solution.py:72
  (244 shorter events, 108.9 us)
Async XLA Ops:
  6.5 548.5 %copy-start = (bf16[512,512]{1,0:T(8,128)(2,1)S(1)}, bf16[512,512]{1,0:T(8,128)(2,1)}, u32[]{:S(2)}) copy-start(bf16[512,512]{1,0:T(8,128)(2,1)} %param.11) | copy-start | bytes 1572868
  6.5 98.3 %all-gather.2.cloned.1.call-start = ((), (), s32[]{:S(2)}) async-start(), calls=%async_computation.1 | async-start | bytes 2359296 | tf_op jit(solution)/shard_map/all_gather | solution.py:54
  9.6 66.2 %copy-start.2 = (bf16[2048,64]{0,1:T(8,128)(2,1)S(1)}, bf16[2048,64]{0,1:T(8,128)(2,1)}, u32[]{:S(2)}) copy-start(bf16[2048,64]{0,1:T(8,128)(2,1)} %param.10) | copy-start | bytes 786436
  9.6 67.0 %copy-start.1 = (s32[64,512]{1,0:T(8,128)S(1)}, s32[64,512]{1,0:T(8,128)}, u32[]{:S(2)}) copy-start(s32[64,512]{1,0:T(8,128)} %param.13) | copy-start | bytes 393220
  9.6 67.1 %copy-start.3 = (s32[64,512]{1,0:T(8,128)S(1)}, s32[64,512]{1,0:T(8,128)}, u32[]{:S(2)}) copy-start(s32[64,512]{1,0:T(8,128)} %param.14) | copy-start | bytes 393220
  76.6 478.4 %reduce-scatter.2.cloned.1.call-start = ((), (), s32[]{:S(2)}) async-start(), calls=%async_computation.2 | async-start | bytes 17301504 | tf_op jit(solution)/shard_map/reduce_scatter | solution.py:72
  309.5 0.7 copy-start.5
  309.5 245.5 %copy-start.4 = (f32[512]{0:T(512)S(1)}, f32[512]{0:T(512)}, u32[]{:S(2)}) copy-start(f32[512]{0:T(512)} %param.12) | copy-start | bytes 6148
Sparse Core Ops, SparseCore 0:
  76.7 28.0 all-gather.1
  309.7 245.2 reduce-scatter.1
where the time goes:
time: 566 us; the launch traced here: 564 us
  local copies, waits for them, and re-layouts  156 us (28%)
  blocking collectives  147 us (26%)
  waiting for transfers between devices  140 us (25%)
  matrix products  100 us (18%)
  between operations  14.2 us (3%)
  other arithmetic  5.7 us (1%)
    gather x16, local copies, waits for them, and re-layouts, tile_sums(): picked = jnp.take(table, source.reshape(-1), axis=0)  147 us
    unnamed x1, blocking collectives  132 us
    reduce_scatter x1, waiting for transfers between devices, body(): lax.psum_scatter(partial_rows, 'col', scatter_dimension=0, tiled=True)  112 us
    dot_general x16, matrix products, tile_sums(): jnp.einsum('gts,gsf->gtf', onehot, picked, preferred_element_type=jnp.flo...  50.3 us
    dot_general x16, matrix products, group_count(): jnp.dot(weights[None, :].astype(jnp.bfloat16), onehot, preferred_element_...  47.8 us
    all_gather x1, waiting for transfers between devices, body(): panel_rows = lax.all_gather(scaled, 'row', axis=1, tiled=True)  28 us
    psum x1, blocking collectives, body(): out_degree = lax.psum(out_local, 'row')  14.9 us
  transfers between devices with their start and end apart: 2, of which 2 were waited for; matrix products, arithmetic and copies ran while one was open for 0% of the time, Pallas kernels for 0%

commit v1 on v0

v1 whole, which is shorter than its diff:
```python
import functools

import jax
import jax.numpy as jnp
from jax import lax
from jax.experimental import pallas as pl
from jax.experimental.pallas import tpu as pltpu
from jax.sharding import PartitionSpec as P

TILE = 128
F = 512
SRC = 2048
CAP = 512
TILES = 64
NROW = 8
NY = 4
NZ = 8
AHEAD = 3
bf16 = jnp.bfloat16
f32 = jnp.float32
f8 = jnp.float8_e4m3fn
MESH = pl.DeviceIdType.MESH
NT = (((1,), (1,)), ((), ()))


def onehot(row, size):
    parts = []
    for base in range(0, size, 256):
        width = min(256, size - base)
        value = (row - base).astype(f32).astype(bf16)
        places = lax.broadcasted_iota(jnp.int32, (width, row.shape[1]), 0).astype(f32).astype(bf16)
        parts.append(jnp.where(places == value, jnp.ones((), bf16), jnp.zeros((), bf16)).astype(f8))
    return parts[0] if len(parts) == 1 else jnp.concatenate(parts, axis=0)


def kernel(
    xt, src, dst, cnt, weight, bias, out,
    xg, xs, deg, deg_in, cin, cin_in, cmid, cmid_in, amat,
    zs, zr, ys, yr, p1, p1_in, p2, p2_in, acc_z, acc_y,
    x_sem, d_sem, c_sem, m_sem, z_sem, y_sem, p1_sem, p2_sem, own_sem,
):
    r = lax.axis_index("row")
    c = lax.axis_index("col")
    y = c // NZ
    z = lax.rem(c, NZ)

    def row_peer(k):
        return (lax.rem(r + k, NROW), c)

    def z_peer(k):
        return (r, y * NZ + lax.rem(z + k, NZ))

    def y_peer(k):
        return (r, lax.rem(y + k, NY) * NZ + z)

    barrier = pltpu.get_barrier_semaphore()
    peers = [row_peer(k) for k in range(1, NROW)]
    peers += [z_peer(k) for k in range(1, NZ)]
    peers += [y_peer(k) for k in range(1, NY)]
    for peer in peers:
        pl.semaphore_signal(barrier, inc=1, device_id=peer, device_id_type=MESH)
    pl.semaphore_wait(barrier, len(peers))

    def remote(source, target, sems, index, peer):
        return pltpu.make_async_remote_copy(
            src_ref=source, dst_ref=target, send_sem=sems.at[(0,) + index],
            recv_sem=sems.at[(1,) + index], device_id=peer, device_id_type=MESH,
        )

    x_copies = [remote(xt, xg.at[r], x_sem, (k - 1,), row_peer(k)) for k in range(1, NROW)]
    for copy in x_copies:
        copy.start()
    own = pltpu.make_async_copy(xt, xg.at[r], own_sem)
    own.start()

    slots = lax.broadcasted_iota(jnp.int32, (1, CAP), 1)

    def edges(t):
        return src[pl.ds(t, 1), :], dst[pl.ds(t, 1), :], slots < cnt[0, t]

    def count_step(zi, total):
        rows = []
        for j in range(8):
            s, d, valid = edges(2 * ((j // 2) * NZ + zi) + j % 2)
            left = jnp.concatenate(
                [onehot(jnp.where(valid, s >> 7, -1), 32), jnp.ones((32, CAP), f8)], axis=0
            )
            right = jnp.concatenate(
                [onehot(s & 127, 128), onehot(jnp.where(valid, d, -1), 128)], axis=0
            )
            both = lax.dot_general(left, right, NT, preferred_element_type=f32)
            total = total + both[:16, :128]
            rows.append(both[32:33, 128:])
        cin[zi] = jnp.concatenate(rows, axis=0)
        return total

    deg[...] = lax.fori_loop(0, NZ, count_step, jnp.zeros((16, 128), f32))
    d_copies = [remote(deg, deg_in.at[k - 1], d_sem, (k - 1,), row_peer(k)) for k in range(1, NROW)]
    for copy in d_copies:
        copy.start()
    c_copies = [
        remote(cin.at[lax.rem(z + k, NZ)], cin_in.at[k - 1], c_sem, (k - 1,), z_peer(k))
        for k in range(1, NZ)
    ]
    for copy in c_copies:
        copy.start()

    def build(t, slot):
        s, d, valid = edges(t)
        place = jnp.where(valid, (s >> 9) * TILE + d, -1)
        count = lax.dot_general(
            onehot(place, 512), onehot(s & 511, 512), NT, preferred_element_type=f32
        )
        base = pl.multiple_of(slot * TILE, TILE)
        for h in range(4):
            amat[pl.ds(base, TILE), h * 512 : (h + 1) * 512] = count[
                h * TILE : (h + 1) * TILE
            ].astype(bf16)

    def build_z(step):
        def one(j, carry):
            for u in range(2):
                jj = 2 * u + j
                zi = lax.rem(z + NZ - 1 - step, NZ) if u == 0 else lax.rem(z + 1 + step, NZ)
                build(2 * (jj * NZ + zi), step * 4 + jj)
            return carry

        lax.fori_loop(0, 2, one, 0)

    def build_y(step):
        def one(j, carry):
            for u in range(2):
                jj = 4 * u + j
                yi = lax.rem(y + NY - 1 - step, NY) if u == 0 else lax.rem(y + 1 + step, NY)
                build(2 * (yi * NZ + jj) + 1, 32 + step * 8 + jj)
            return carry

        lax.fori_loop(0, 4, one, 0)

    def build_step(step):
        build_z(step)

        @pl.when(lax.rem(step, 2) == 0)
        def _():
            build_y(step // 2)

    def ahead(step, carry):
        build_step(step)
        return carry

    lax.fori_loop(0, AHEAD, ahead, 0)

    for copy in d_copies:
        copy.wait()
    total = deg[...]
    for k in range(1, NROW):
        total = total + deg_in[k - 1]
    scale = lax.rsqrt(1.0 + total)
    for copy in c_copies:
        copy.wait()
    mid = cin[z]
    for k in range(1, NZ):
        mid = mid + cin_in[k - 1]
    cmid[...] = mid
    m_copies = [remote(cmid, cmid_in.at[k - 1], m_sem, (k - 1,), y_peer(k)) for k in range(1, NY)]
    for copy in m_copies:
        copy.start()
    for copy in x_copies:
        copy.wait()
    own.wait()

    def scale_rows(i, carry):
        base = pl.multiple_of(i * 64, 64)
        for h in range(16):
            cols = slice(h * 128, (h + 1) * 128)
            xs[pl.ds(base, 64), cols] = (xg[i, :, cols].astype(f32) * scale[h : h + 1, :]).astype(bf16)
        return carry

    lax.fori_loop(0, NROW, scale_rows, 0)

    def z_copy(d, s):
        return remote(zs.at[d, s], zr.at[d, s], z_sem, (d, s), z_peer(1 if d == 0 else NZ - 1))

    def y_copy(d, s):
        return remote(ys.at[d, s], yr.at[d, s], y_sem, (d, s), y_peer(1 if d == 0 else NY - 1))

    def product(slot, tiles):
        base = pl.multiple_of(slot * TILE, TILE)
        return lax.dot_general(
            amat[pl.ds(base, tiles * TILE), :], xs[...], NT, preferred_element_type=f32
        )

    p2_copies = [
        remote(p2.at[lax.rem(z + k, NZ)], p2_in.at[k - 1], p2_sem, (k - 1,), z_peer(k))
        for k in range(1, NZ)
    ]
    p1_copies = [
        remote(p1.at[lax.rem(y + k, NY)], p1_in.at[k - 1], p1_sem, (k - 1,), y_peer(k))
        for k in range(1, NY)
    ]

    def ring_step(step, carry):
        for d in range(2):
            acc_z[...] = product(step * 4 + 2 * d, 2)

            @pl.when(step > 0)
            def _():
                z_copy(d, step - 1).wait_recv()
                acc_z[...] += zr[d, step - 1].astype(f32)

            @pl.when(step < NZ - 1)
            def _():
                zs[d, step] = acc_z[...].astype(bf16)
                z_copy(d, step).start()

            @pl.when(step == NZ - 1)
            def _():
                for u in range(2):
                    p1[2 * d + u] = acc_z[u * TILE : (u + 1) * TILE].astype(bf16)

        @pl.when(lax.rem(step, 2) == 0)
        def _():
            q = step // 2
            for d in range(2):
                acc_y[...] = product(32 + q * 8 + 4 * d, 4)

                @pl.when(q > 0)
                def _():
                    y_copy(d, q - 1).wait_recv()
                    acc_y[...] += yr[d, q - 1].astype(f32)

                @pl.when(q < NY - 1)
                def _():
                    ys[d, q] = acc_y[...].astype(bf16)
                    y_copy(d, q).start()

                @pl.when(q == NY - 1)
                def _():
                    for u in range(4):
                        p2[4 * d + u] = acc_y[u * TILE : (u + 1) * TILE].astype(bf16)

            @pl.when(q == NY - 1)
            def _():
                for copy in p2_copies:
                    copy.start()

        @pl.when(step + AHEAD < NZ)
        def _():
            build_step(step + AHEAD)

        return carry

    lax.fori_loop(0, NZ, ring_step, 0)
    for copy in p1_copies:
        copy.start()

    for copy in m_copies:
        copy.wait()
    degree = cmid[pl.ds(2 * y, 2), :]
    for k in range(1, NY):
        degree = degree + cmid_in[k - 1, pl.ds(2 * y, 2), :]
    norm = jnp.transpose(lax.rsqrt(1.0 + jnp.concatenate([degree] * 4, axis=0)))

    def finish(half, total):
        normed = (total * norm[:, half : half + 1]).astype(bf16)
        result = jnp.dot(normed, weight[...], preferred_element_type=f32) + bias[...]
        out[half * TILE : (half + 1) * TILE, :] = jnp.maximum(result, 0.0).astype(bf16)

    for copy in p1_copies:
        copy.wait()
    total = p1[y].astype(f32)
    for k in range(1, NY):
        total = total + p1_in[k - 1].astype(f32)
    finish(0, total)
    for copy in p2_copies:
        copy.wait()
    total = p2[z].astype(f32)
    for k in range(1, NZ):
        total = total + p2_in[k - 1].astype(f32)
    finish(1, total)

    def drain(step, carry):
        for d in range(2):
            z_copy(d, step).wait_send()
        return carry

    lax.fori_loop(0, NZ - 1, drain, 0)

    def drain_y(step, carry):
        for d in range(2):
            y_copy(d, step).wait_send()
        return carry

    lax.fori_loop(0, NY - 1, drain_y, 0)


def body(features, weight, bias, edge_src, edge_dst, tile_count):
    vmem = pl.BlockSpec(memory_space=pltpu.VMEM)
    smem = pl.BlockSpec(memory_space=pltpu.SMEM)
    units = features.shape[1]
    dma = pltpu.SemaphoreType.DMA
    return pl.pallas_call(
        kernel,
        out_shape=jax.ShapeDtypeStruct((2 * TILE, F), bf16),
        in_specs=[vmem, vmem, vmem, smem, vmem, vmem],
        out_specs=vmem,
        scratch_shapes=[
            pltpu.VMEM((NROW, units, SRC), bf16),
            pltpu.VMEM((F, SRC), bf16),
            pltpu.VMEM((16, 128), f32),
            pltpu.VMEM((NROW - 1, 16, 128), f32),
            pltpu.VMEM((NZ, 8, 128), f32),
            pltpu.VMEM((NZ - 1, 8, 128), f32),
            pltpu.VMEM((8, 128), f32),
            pltpu.VMEM((NY - 1, 8, 128), f32),
            pltpu.VMEM((TILES * TILE, SRC), bf16),
            pltpu.VMEM((2, NZ - 1, 2 * TILE, F), bf16),
            pltpu.VMEM((2, NZ - 1, 2 * TILE, F), bf16),
            pltpu.VMEM((2, NY - 1, 4 * TILE, F), bf16),
            pltpu.VMEM((2, NY - 1, 4 * TILE, F), bf16),
            pltpu.VMEM((NY, TILE, F), bf16),
            pltpu.VMEM((NY - 1, TILE, F), bf16),
            pltpu.VMEM((NZ, TILE, F), bf16),
            pltpu.VMEM((NZ - 1, TILE, F), bf16),
            pltpu.VMEM((2 * TILE, F), f32),
            pltpu.VMEM((4 * TILE, F), f32),
            dma((2, NROW - 1)),
            dma((2, NROW - 1)),
            dma((2, NZ - 1)),
            dma((2, NY - 1)),
            dma((2, 2, NZ - 1)),
            dma((2, 2, NY - 1)),
            dma((2, NY - 1)),
            dma((2, NZ - 1)),
            dma,
        ],
        compiler_params=pltpu.CompilerParams(
            collective_id=0, has_side_effects=True, vmem_limit_bytes=60 * 1024 * 1024
        ),
        name="graph_layer",
    )(features.T, edge_src, edge_dst, tile_count.T, weight, bias[None, :])


def solution(mesh):
    in_specs = (P("col", "row"), P(), P(), P("row", "col"), P("row", "col"), P("row", "col"))
    out_specs = P(("row", "col"), None)
    return jax.shard_map(body, mesh=mesh, in_specs=in_specs, out_specs=out_specs, check_vma=False)
```

time: 566 us -> 112 us (0.20)
  local copies, waits for them, and re-layouts: 156 us -> 1.67 us
  blocking collectives: 147 us -> 0 us
  waiting for transfers between devices: 140 us -> 0 us
  Pallas kernels: 0 us -> 108 us
  matrix products: 100 us -> 0 us
  between operations: 14.2 us -> 0.01 us
  other arithmetic: 5.7 us -> 0 us
    gather x16 -> x0, local copies, waits for them, and re-layouts: 147 us -> none  [tile_sums(): picked = jnp.take(table, source.reshape(-1), axis=0)]
    unnamed x1 -> x0, blocking collectives: 132 us -> none
    reduce_scatter x1 -> x0, waiting for transfers between devices: 112 us -> none  [body(): lax.psum_scatter(partial_rows, 'col', scatter_dimension=0, tiled=True)]
    pallas_call x0 -> x1, Pallas kernels: none -> 108 us  [body(): pl.pallas_call(kernel, out_shape=jax.ShapeDtypeStruct((2 * TILE, F), bf16...]
    dot_general x33 -> x0, matrix products: 100 us -> none  [the longest x16 50.3 us: tile_sums(): jnp.einsum('gts,gsf->gtf', onehot, picked, preferred_element_type=jnp.flo...]
    all_gather x1 -> x0, waiting for transfers between devices: 28 us -> none  [body(): panel_rows = lax.all_gather(scaled, 'row', axis=1, tiled=True)]
    psum x1 -> x0, blocking collectives: 14.9 us -> none  [body(): out_degree = lax.psum(out_local, 'row')]
  transfers between devices with their start and end apart: 2 -> 0, of which waited for: 2 -> 0; matrix products, arithmetic and copies ran while one was open for 0% -> 0% of each run, Pallas kernels for 0% -> 0%
where the time goes in v1:
time: 112 us; the launch traced here: 110 us
  Pallas kernels  108 us (96%)
  local copies, waits for them, and re-layouts  1.67 us (1%)
    pallas_call x1, Pallas kernels, body(): pl.pallas_call(kernel, out_shape=jax.ShapeDtypeStruct((2 * TILE, F), bf16...  108 us

profile of v1, /device:TPU:8, one launch (start us, length us, event | category | flops | bytes accessed | tf_op | source)
XLA Modules:
  0.0 109.8 jit_solution(10422474610618554941)
XLA Ops:
  0.0 108.1 %graph_layer.1 = bf16[256,512]{1,0:T(8,128)(2,1)} custom-call(bf16[64,2048]{1,0:T(8,128)(2,1)} %bitcast.3, s32[64,512]{1,0:T(8,128)} %src.1, s32[64,512]{1,0:T(8,128)} %dst.1, s32[1,64]{1,0:T(1,128)} %bitcast.5, bf16[512,512]{1,0:T(8,128)(2,1)} %weight.1, f32[1,512]{1,0:T(1,128)} %bitcast.4), custom_call_target="tpu_custom_call" | custom-call | tf_op jit(solution)/shard_map/graph_layer/pallas_call | solution.py:302
  108.1 1.7 %copy.8 = bf16[256,512]{1,0:T(8,128)(2,1)} copy(bf16[256,512]{1,0:T(8,128)(2,1)} %graph_layer.1) | data formatting | bytes 524288

commit v2 on v1

v2 whole, which is shorter than its diff:
```python
import functools

import jax
import jax.numpy as jnp
from jax import lax
from jax.experimental import pallas as pl
from jax.experimental.pallas import tpu as pltpu
from jax.sharding import PartitionSpec as P

TILE = 128
F = 512
SRC = 2048
CAP = 512
TILES = 64
NROW = 8
NY = 4
NZ = 8
AHEAD = 2
HALF = 64
STEP = 1024
bf16 = jnp.bfloat16
f32 = jnp.float32
f8 = jnp.float8_e4m3fn
MESH = pl.DeviceIdType.MESH
NT = (((1,), (1,)), ((), ()))


def onehot(row, size):
    parts = []
    for base in range(0, size, 256):
        width = min(256, size - base)
        value = (row - base).astype(f32).astype(bf16)
        places = lax.broadcasted_iota(jnp.int32, (width, row.shape[1]), 0).astype(f32).astype(bf16)
        parts.append(jnp.where(places == value, jnp.ones((), bf16), jnp.zeros((), bf16)).astype(f8))
    return parts[0] if len(parts) == 1 else jnp.concatenate(parts, axis=0)


def kernel(
    xt, src, dst, cnt, weight, bias, out,
    xg, xs, deg, deg_in, cin, cin_in, cmid, cmid_in, amat,
    zs, zr, ys, yr, p1, p1_in, p2, p2_out, p2_in, acc,
    x_sem, d_sem, c_sem, m_sem, z_sem, y_sem, p1_sem, p2_sem, own_sem,
):
    r = lax.axis_index("row")
    c = lax.axis_index("col")
    y = c // NZ
    z = lax.rem(c, NZ)

    def row_peer(k):
        return (lax.rem(r + k, NROW), c)

    def z_peer(k):
        return (r, y * NZ + lax.rem(z + k, NZ))

    def y_peer(k):
        return (r, lax.rem(y + k, NY) * NZ + z)

    barrier = pltpu.get_barrier_semaphore()
    peers = [row_peer(k) for k in range(1, NROW)]
    peers += [z_peer(k) for k in range(1, NZ)]
    peers += [y_peer(k) for k in range(1, NY)]
    for peer in peers:
        pl.semaphore_signal(barrier, inc=1, device_id=peer, device_id_type=MESH)
    pl.semaphore_wait(barrier, len(peers))

    def remote(source, target, sems, index, peer):
        return pltpu.make_async_remote_copy(
            src_ref=source, dst_ref=target, send_sem=sems.at[(0,) + index],
            recv_sem=sems.at[(1,) + index], device_id=peer, device_id_type=MESH,
        )

    after, before, opposite = (lax.rem(r + k, NROW) for k in (2, 6, 4))
    sibling = (r + 1 - 2 * lax.rem(r, 2), c)
    low, high = pl.ds(0, 32), pl.ds(32, 32)

    def x_copy(index, source, target, peer):
        return remote(source, target, x_sem, (index,), peer)

    right_low = x_copy(0, xt.at[low], xg.at[r, low], (after, c))
    left_high = x_copy(1, xt.at[high], xg.at[r, high], (before, c))
    right_high = x_copy(2, xt.at[high], xg.at[r, high], (after, c))
    left_low = x_copy(3, xt.at[low], xg.at[r, low], (before, c))
    own_across = x_copy(4, xt, xg.at[r], sibling)
    on_right = x_copy(5, xg.at[before, low], xg.at[before, low], (after, c))
    on_left = x_copy(6, xg.at[after, high], xg.at[after, high], (before, c))
    before_across = x_copy(7, xg.at[before], xg.at[before], sibling)
    after_across = x_copy(8, xg.at[after], xg.at[after], sibling)
    opposite_across = x_copy(9, xg.at[opposite], xg.at[opposite], sibling)
    for copy in (right_low, left_high, right_high, left_low, own_across):
        copy.start()
    own = pltpu.make_async_copy(xt, xg.at[r], own_sem)
    own.start()

    slots = lax.broadcasted_iota(jnp.int32, (1, CAP), 1)

    def edges(t):
        return src[pl.ds(t, 1), :], dst[pl.ds(t, 1), :], slots < cnt[0, t]

    def count_step(zi, total):
        rows = []
        for j in range(8):
            s, d, valid = edges(2 * ((j // 2) * NZ + zi) + j % 2)
            left = jnp.concatenate(
                [onehot(jnp.where(valid, s >> 7, -1), 32), jnp.ones((32, CAP), f8)], axis=0
            )
            right = jnp.concatenate(
                [onehot(s & 127, 128), onehot(jnp.where(valid, d, -1), 128)], axis=0
            )
            both = lax.dot_general(left, right, NT, preferred_element_type=f32)
            total = total + both[:16, :128]
            rows.append(both[32:33, 128:])
        cin[zi] = jnp.concatenate(rows, axis=0)
        return total

    deg[...] = lax.fori_loop(0, NZ // 2, count_step, jnp.zeros((16, 128), f32))
    right_low.wait_recv()
    on_right.start()
    left_high.wait_recv()
    on_left.start()
    deg[...] = lax.fori_loop(NZ // 2, NZ, count_step, deg[...])
    d_copies = [remote(deg, deg_in.at[k - 1], d_sem, (k - 1,), row_peer(k)) for k in range(1, NROW)]
    for copy in d_copies:
        copy.start()
    c_copies = [
        remote(cin.at[lax.rem(z + k, NZ)], cin_in.at[k - 1], c_sem, (k - 1,), z_peer(k))
        for k in range(1, NZ)
    ]
    for copy in c_copies:
        copy.start()
    right_high.wait_recv()
    before_across.start()
    left_low.wait_recv()
    after_across.start()

    def count_matrix(t):
        s, d, valid = edges(t)
        place = jnp.where(valid, (s >> 9) * TILE + d, -1)
        return lax.dot_general(
            onehot(place, 512), onehot(s & 511, 512), NT, preferred_element_type=f32
        ).astype(bf16)

    def build_z(step):
        def one(j, carry):
            for u in range(2):
                jj = 2 * u + j
                zi = lax.rem(z + NZ - 1 - step, NZ) if u == 0 else lax.rem(z + 1 + step, NZ)
                count = count_matrix(2 * (jj * NZ + zi))
                base = pl.multiple_of(step * STEP + jj * TILE, TILE)
                for h in range(4):
                    amat[pl.ds(base, TILE), h * 512 : (h + 1) * 512] = count[
                        h * TILE : (h + 1) * TILE
                    ]
            return carry

        lax.fori_loop(0, 2, one, 0)

    def build_y(group):
        q = group // 2
        d = lax.rem(group, 2)
        yi = lax.rem(y + 2 * NY + (2 * d - 1) * (q + 1), NY)

        def one(j, carry):
            for u in range(2):
                jj = 2 * j + u
                count = count_matrix(2 * (yi * NZ + 4 * d + jj) + 1)
                for part in range(2):
                    base = pl.multiple_of((2 * q + part) * STEP + 512 + d * 256 + jj * HALF, HALF)
                    for h in range(4):
                        start = h * TILE + part * HALF
                        amat[pl.ds(base, HALF), h * 512 : (h + 1) * 512] = count[
                            start : start + HALF
                        ]
            return carry

        lax.fori_loop(0, 2, one, 0)

    def ahead(step, carry):
        build_z(step)
        build_y(step + 1)
        return carry

    build_y(0)
    lax.fori_loop(0, AHEAD - 1, ahead, 0)
    on_right.wait_recv()
    on_left.wait_recv()
    opposite_across.start()
    lax.fori_loop(AHEAD - 1, AHEAD, ahead, 0)

    for copy in d_copies:
        copy.wait()
    total = deg[...]
    for k in range(1, NROW):
        total = total + deg_in[k - 1]
    scale = lax.rsqrt(1.0 + total)
    for copy in c_copies:
        copy.wait()
    mid = cin[z]
    for k in range(1, NZ):
        mid = mid + cin_in[k - 1]
    cmid[...] = mid
    m_copies = [remote(cmid, cmid_in.at[k - 1], m_sem, (k - 1,), y_peer(k)) for k in range(1, NY)]
    for copy in m_copies:
        copy.start()
    for copy in (own_across, before_across, after_across, opposite_across):
        copy.wait_recv()
    own.wait()

    def scale_rows(i, carry):
        base = pl.multiple_of(i * 64, 64)
        for h in range(16):
            cols = slice(h * 128, (h + 1) * 128)
            xs[pl.ds(base, 64), cols] = (xg[i, :, cols].astype(f32) * scale[h : h + 1, :]).astype(bf16)
        return carry

    lax.fori_loop(0, NROW, scale_rows, 0)

    def product(step):
        def one(i, carry):
            base = pl.multiple_of(step * STEP + i * 512, 512)
            acc[pl.ds(pl.multiple_of(i * 512, 512), 512), :] = lax.dot_general(
                amat[pl.ds(base, 512), :], xs[...], NT, preferred_element_type=f32
            )
            return carry

        lax.fori_loop(0, 2, one, 0)

    def z_copy(d, s, u):
        rows = pl.ds(u * TILE, TILE)
        return remote(
            zs.at[d, lax.rem(s, 2), rows], zr.at[d, s, rows], z_sem, (d, s, u),
            z_peer(1 if d == 0 else NZ - 1),
        )

    def y_copy(d, s):
        return remote(ys.at[d, s], yr.at[d, s], y_sem, (d, s), y_peer(1 if d == 0 else NY - 1))

    def z_add(d, s, u):
        z_copy(d, s - 1, u).wait_recv()
        rows = slice(d * 256 + u * TILE, d * 256 + (u + 1) * TILE)
        acc[rows] += zr[d, s - 1, u * TILE : (u + 1) * TILE].astype(f32)

    def z_part(d, s, u):
        @pl.when(s > 0)
        def _():
            z_add(d, s, u)

        @pl.when(s > 1)
        def _():
            z_copy(d, s - 2, u).wait_send()

        rows = slice(d * 256 + u * TILE, d * 256 + (u + 1) * TILE)
        zs[d, lax.rem(s, 2), u * TILE : (u + 1) * TILE] = acc[rows].astype(bf16)
        z_copy(d, s, u).start()

    def y_part(d, s):
        rows = slice(512 + d * 256, 768 + d * 256)

        @pl.when(s > 1)
        def _():
            y_copy(d, s - 2).wait_recv()
            acc[rows] += yr[d, s - 2].astype(f32)

        ys[d, s] = acc[rows].astype(bf16)
        y_copy(d, s).start()

    def y_last(part):
        for d in range(2):
            y_copy(d, 4 + part).wait_recv()
            for u in range(4):
                first = 512 + d * 256 + u * HALF
                p2[part, 4 * d + u] = acc[first : first + HALF] + yr[
                    d, 4 + part, u * HALF : (u + 1) * HALF
                ].astype(f32)

    def p2_copy(part, slot):
        return remote(
            p2_out.at[part, slot], p2_in.at[part, slot], p2_sem, (part, slot),
            z_peer(1 if slot < 4 else NZ - 1),
        )

    def p2_hop(part, hop):
        for slot in (hop, 4 + hop) if hop < 3 else (hop,):
            zi = lax.rem(z + (4 - hop if slot < 4 else 5 + hop), NZ)
            value = p2[part, zi]
            if hop > 0:
                p2_copy(part, slot - 1).wait_recv()
                value = value + p2_in[part, slot - 1].astype(f32)
            p2_out[part, slot] = value.astype(bf16)
            p2_copy(part, slot).start()

    def ring_step(s, carry):
        product(s)

        @pl.when(s + AHEAD < NZ)
        def _():
            build_z(s + AHEAD)

        @pl.when(s + AHEAD + 1 < NZ)
        def _():
            build_y(s + AHEAD + 1)

        for d in range(2):
            z_part(d, s, 0)

        @pl.when(s < 6)
        def _():
            for d in range(2):
                y_part(d, s)

        for d in range(2):
            z_part(d, s, 1)
        return carry

    lax.fori_loop(0, NZ - 1, ring_step, 0)
    y_last(0)
    p2_hop(0, 0)
    product(NZ - 1)
    p2_hop(0, 1)
    y_last(1)
    p2_hop(1, 0)
    p2_hop(0, 2)
    p1_copies = [
        remote(p1.at[lax.rem(y + k, NY)], p1_in.at[k - 1], p1_sem, (k - 1,), y_peer(k))
        for k in range(1, NY)
    ]
    for u in range(2):
        for d in range(2):
            z_add(d, NZ - 1, u)
            first = (2 * d + u) * TILE
            p1[2 * d + u] = acc[first : first + TILE].astype(bf16)
    for copy in p1_copies:
        copy.start()
    p2_hop(1, 1)
    p2_hop(0, 3)
    p2_hop(1, 2)
    p2_hop(1, 3)

    for copy in m_copies:
        copy.wait()
    degree = cmid[pl.ds(2 * y, 2), :]
    for k in range(1, NY):
        degree = degree + cmid_in[k - 1, pl.ds(2 * y, 2), :]
    norm = jnp.transpose(lax.rsqrt(1.0 + jnp.concatenate([degree] * 4, axis=0)))

    def finish(half, total):
        normed = (total * norm[:, half : half + 1]).astype(bf16)
        result = jnp.dot(normed, weight[...], preferred_element_type=f32) + bias[...]
        out[half * TILE : (half + 1) * TILE, :] = jnp.maximum(result, 0.0).astype(bf16)

    for copy in p1_copies:
        copy.wait()
    total = acc[pl.ds(pl.multiple_of(y * TILE, TILE), TILE), :]
    for k in range(1, NY):
        total = total + p1_in[k - 1].astype(f32)
    finish(0, total)
    totals = []
    for part in range(2):
        total = p2[part, z]
        for slot in (3, 6):
            p2_copy(part, slot).wait_recv()
            total = total + p2_in[part, slot].astype(f32)
        totals.append(total)
    finish(1, jnp.concatenate(totals, axis=0))

    for copy in (
        right_low, left_high, right_high, left_low, own_across,
        on_right, on_left, before_across, after_across, opposite_across,
    ):
        copy.wait_send()
    for d in range(2):
        for s in (NZ - 3, NZ - 2):
            for u in range(2):
                z_copy(d, s, u).wait_send()
        for s in range(6):
            y_copy(d, s).wait_send()
    for part in range(2):
        for slot in range(7):
            p2_copy(part, slot).wait_send()


def body(features, weight, bias, edge_src, edge_dst, tile_count):
    vmem = pl.BlockSpec(memory_space=pltpu.VMEM)
    smem = pl.BlockSpec(memory_space=pltpu.SMEM)
    units = features.shape[1]
    dma = pltpu.SemaphoreType.DMA
    return pl.pallas_call(
        kernel,
        out_shape=jax.ShapeDtypeStruct((2 * TILE, F), bf16),
        in_specs=[vmem, vmem, vmem, smem, vmem, vmem],
        out_specs=vmem,
        scratch_shapes=[
            pltpu.VMEM((NROW, units, SRC), bf16),
            pltpu.VMEM((F, SRC), bf16),
            pltpu.VMEM((16, 128), f32),
            pltpu.VMEM((NROW - 1, 16, 128), f32),
            pltpu.VMEM((NZ, 8, 128), f32),
            pltpu.VMEM((NZ - 1, 8, 128), f32),
            pltpu.VMEM((8, 128), f32),
            pltpu.VMEM((NY - 1, 8, 128), f32),
            pltpu.VMEM((TILES * TILE, SRC), bf16),
            pltpu.VMEM((2, 2, 2 * TILE, F), bf16),
            pltpu.VMEM((2, NZ - 1, 2 * TILE, F), bf16),
            pltpu.VMEM((2, 6, 2 * TILE, F), bf16),
            pltpu.VMEM((2, 6, 2 * TILE, F), bf16),
            pltpu.VMEM((NY, TILE, F), bf16),
            pltpu.VMEM((NY - 1, TILE, F), bf16),
            pltpu.VMEM((2, NZ, HALF, F), f32),
            pltpu.VMEM((2, 7, HALF, F), bf16),
            pltpu.VMEM((2, 7, HALF, F), bf16),
            pltpu.VMEM((STEP, F), f32),
            dma((2, 10)),
            dma((2, NROW - 1)),
            dma((2, NZ - 1)),
            dma((2, NY - 1)),
            dma((2, 2, NZ - 1, 2)),
            dma((2, 2, 6)),
            dma((2, NY - 1)),
            dma((2, 2, 7)),
            dma,
        ],
        compiler_params=pltpu.CompilerParams(
            collective_id=0, has_side_effects=True, vmem_limit_bytes=60 * 1024 * 1024
        ),
        name="graph_layer",
    )(features.T, edge_src, edge_dst, tile_count.T, weight, bias[None, :])


def solution(mesh):
    in_specs = (P("col", "row"), P(), P(), P("row", "col"), P("row", "col"), P("row", "col"))
    out_specs = P(("row", "col"), None)
    return jax.shard_map(body, mesh=mesh, in_specs=in_specs, out_specs=out_specs, check_vma=False)
```

time: 112 us -> 91.3 us (0.82); the launches traced: 110 us -> 91.2 us
  Pallas kernels: 108 us -> 89.5 us
    pallas_call x1, Pallas kernels: 108 us -> 89.5 us  [body(): pl.pallas_call(kernel, out_shape=jax.ShapeDtypeStruct((2 * TILE, F), bf16...]
where the time goes in v2:
time: 91.3 us; the launch traced here: 91.2 us
  Pallas kernels  89.5 us (98%)
  local copies, waits for them, and re-layouts  1.67 us (2%)
    pallas_call x1, Pallas kernels, body(): pl.pallas_call(kernel, out_shape=jax.ShapeDtypeStruct((2 * TILE, F), bf16...  89.5 us

profile of v2, /device:TPU:8, one launch (start us, length us, event | category | flops | bytes accessed | tf_op | source)
XLA Modules:
  0.0 91.2 jit_solution(71789447746183477)
XLA Ops:
  0.0 89.5 %graph_layer.1 = bf16[256,512]{1,0:T(8,128)(2,1)} custom-call(bf16[64,2048]{1,0:T(8,128)(2,1)} %bitcast.3, s32[64,512]{1,0:T(8,128)} %src.1, s32[64,512]{1,0:T(8,128)} %dst.1, s32[1,64]{1,0:T(1,128)} %bitcast.5, bf16[512,512]{1,0:T(8,128)(2,1)} %weight.1, f32[1,512]{1,0:T(1,128)} %bitcast.4), custom_call_target="tpu_custom_call" | custom-call | tf_op jit(solution)/shard_map/graph_layer/pallas_call | solution.py:386
  89.5 1.7 %copy.8 = bf16[256,512]{1,0:T(8,128)(2,1)} copy(bf16[256,512]{1,0:T(8,128)(2,1)} %graph_layer.1) | data formatting | bytes 524288

commit v3 on v2

--- a/solution.py
+++ b/solution.py
@@ -15,8 +15,8 @@
 NROW = 8
 NY = 4
 NZ = 8
-AHEAD = 2
 HALF = 64
+AHEAD = 3
 STEP = 1024
 bf16 = jnp.bfloat16
 f32 = jnp.float32
@@ -96,42 +96,37 @@
     def edges(t):
         return src[pl.ds(t, 1), :], dst[pl.ds(t, 1), :], slots < cnt[0, t]
 
-    def count_step(zi, total):
-        rows = []
+    def source_step(i, total):
         for j in range(8):
-            s, d, valid = edges(2 * ((j // 2) * NZ + zi) + j % 2)
-            left = jnp.concatenate(
-                [onehot(jnp.where(valid, s >> 7, -1), 32), jnp.ones((32, CAP), f8)], axis=0
-            )
-            right = jnp.concatenate(
-                [onehot(s & 127, 128), onehot(jnp.where(valid, d, -1), 128)], axis=0
-            )
-            both = lax.dot_general(left, right, NT, preferred_element_type=f32)
-            total = total + both[:16, :128]
-            rows.append(both[32:33, 128:])
-        cin[zi] = jnp.concatenate(rows, axis=0)
+            s, _, valid = edges(i * 8 + j)
+            left = onehot(jnp.where(valid, s >> 6, -1), 32)
+            total = total + lax.dot_general(left, onehot(s & 63, 64), NT, preferred_element_type=f32)
         return total
 
-    deg[...] = lax.fori_loop(0, NZ // 2, count_step, jnp.zeros((16, 128), f32))
+    deg[...] = lax.fori_loop(0, TILES // 8, source_step, jnp.zeros((32, 64), f32))
+    d_copies = [remote(deg, deg_in.at[k - 1], d_sem, (k - 1,), row_peer(k)) for k in range(1, NROW)]
+    for copy in d_copies:
+        copy.start()
     right_low.wait_recv()
     on_right.start()
     left_high.wait_recv()
     on_left.start()
-    deg[...] = lax.fori_loop(NZ // 2, NZ, count_step, deg[...])
-    d_copies = [remote(deg, deg_in.at[k - 1], d_sem, (k - 1,), row_peer(k)) for k in range(1, NROW)]
-    for copy in d_copies:
-        copy.start()
+
+    def target_step(zi):
+        rows = []
+        for j in range(8):
+            _, d, valid = edges(2 * ((j // 2) * NZ + zi) + j % 2)
+            right = onehot(jnp.where(valid, d, -1), 128)
+            rows.append(
+                lax.dot_general(jnp.ones((32, CAP), f8), right, NT, preferred_element_type=f32)[:1]
+            )
+        cin[zi] = jnp.concatenate(rows, axis=0)
+
     c_copies = [
         remote(cin.at[lax.rem(z + k, NZ)], cin_in.at[k - 1], c_sem, (k - 1,), z_peer(k))
         for k in range(1, NZ)
     ]
-    for copy in c_copies:
-        copy.start()
-    right_high.wait_recv()
-    before_across.start()
-    left_low.wait_recv()
-    after_across.start()
-
+    m_copies = [remote(cmid, cmid_in.at[k - 1], m_sem, (k - 1,), y_peer(k)) for k in range(1, NY)]
     def count_matrix(t):
         s, d, valid = edges(t)
         place = jnp.where(valid, (s >> 9) * TILE + d, -1)
@@ -140,89 +135,79 @@
         ).astype(bf16)
 
     def build_z(step):
-        def one(j, carry):
-            for u in range(2):
-                jj = 2 * u + j
-                zi = lax.rem(z + NZ - 1 - step, NZ) if u == 0 else lax.rem(z + 1 + step, NZ)
-                count = count_matrix(2 * (jj * NZ + zi))
-                base = pl.multiple_of(step * STEP + jj * TILE, TILE)
-                for h in range(4):
-                    amat[pl.ds(base, TILE), h * 512 : (h + 1) * 512] = count[
-                        h * TILE : (h + 1) * TILE
-                    ]
-            return carry
-
-        lax.fori_loop(0, 2, one, 0)
+        for jj in range(4):
+            zi = lax.rem(z + NZ - 1 - step, NZ) if jj < 2 else lax.rem(z + 1 + step, NZ)
+            count = count_matrix(2 * (jj * NZ + zi))
+            base = pl.multiple_of(step * STEP + jj * TILE, TILE)
+            for h in range(4):
+                amat[pl.ds(base, TILE), h * 512 : (h + 1) * 512] = count[h * TILE : (h + 1) * TILE]
 
     def build_y(group):
         q = group // 2
         d = lax.rem(group, 2)
         yi = lax.rem(y + 2 * NY + (2 * d - 1) * (q + 1), NY)
-
-        def one(j, carry):
-            for u in range(2):
-                jj = 2 * j + u
-                count = count_matrix(2 * (yi * NZ + 4 * d + jj) + 1)
-                for part in range(2):
-                    base = pl.multiple_of((2 * q + part) * STEP + 512 + d * 256 + jj * HALF, HALF)
-                    for h in range(4):
-                        start = h * TILE + part * HALF
-                        amat[pl.ds(base, HALF), h * 512 : (h + 1) * 512] = count[
-                            start : start + HALF
-                        ]
-            return carry
-
-        lax.fori_loop(0, 2, one, 0)
+        for jj in range(4):
+            count = count_matrix(2 * (yi * NZ + 4 * d + jj) + 1)
+            for part in range(2):
+                base = pl.multiple_of((2 * q + part) * STEP + 512 + d * 256 + jj * HALF, HALF)
+                for h in range(4):
+                    start = h * TILE + part * HALF
+                    amat[pl.ds(base, HALF), h * 512 : (h + 1) * 512] = count[start : start + HALF]
 
     def ahead(step, carry):
+        @pl.when(step == 0)
+        def _():
+            right_high.wait_recv()
+            before_across.start()
+            left_low.wait_recv()
+            after_across.start()
+
         build_z(step)
         build_y(step + 1)
+
+        @pl.when(step == 0)
+        def _():
+            on_right.wait_recv()
+            on_left.wait_recv()
+            opposite_across.start()
+
         return carry
 
     build_y(0)
-    lax.fori_loop(0, AHEAD - 1, ahead, 0)
-    on_right.wait_recv()
-    on_left.wait_recv()
-    opposite_across.start()
-    lax.fori_loop(AHEAD - 1, AHEAD, ahead, 0)
-
+    lax.fori_loop(0, AHEAD, ahead, 0)
     for copy in d_copies:
         copy.wait()
     total = deg[...]
     for k in range(1, NROW):
         total = total + deg_in[k - 1]
     scale = lax.rsqrt(1.0 + total)
-    for copy in c_copies:
-        copy.wait()
-    mid = cin[z]
-    for k in range(1, NZ):
-        mid = mid + cin_in[k - 1]
-    cmid[...] = mid
-    m_copies = [remote(cmid, cmid_in.at[k - 1], m_sem, (k - 1,), y_peer(k)) for k in range(1, NY)]
-    for copy in m_copies:
-        copy.start()
+    scale = [
+        jnp.concatenate([scale[2 * h : 2 * h + 1], scale[2 * h + 1 : 2 * h + 2]], axis=1)
+        for h in range(16)
+    ]
+    own.wait()
+
+    def scale_rows(offset):
+        def one(i, carry):
+            piece = lax.rem(offset + 2 * i, NROW)
+            base = pl.multiple_of(piece * 64, 64)
+            for h in range(16):
+                cols = slice(h * 128, (h + 1) * 128)
+                xs[pl.ds(base, 64), cols] = (xg[piece, :, cols].astype(f32) * scale[h]).astype(bf16)
+            return carry
+
+        lax.fori_loop(0, 4, one, 0)
+
+    scale_rows(r)
     for copy in (own_across, before_across, after_across, opposite_across):
         copy.wait_recv()
-    own.wait()
-
-    def scale_rows(i, carry):
-        base = pl.multiple_of(i * 64, 64)
-        for h in range(16):
-            cols = slice(h * 128, (h + 1) * 128)
-            xs[pl.ds(base, 64), cols] = (xg[i, :, cols].astype(f32) * scale[h : h + 1, :]).astype(bf16)
-        return carry
-
-    lax.fori_loop(0, NROW, scale_rows, 0)
+    scale_rows(r + 1)
 
     def product(step):
-        def one(i, carry):
-            base = pl.multiple_of(step * STEP + i * 512, 512)
-            acc[pl.ds(pl.multiple_of(i * 512, 512), 512), :] = lax.dot_general(
-                amat[pl.ds(base, 512), :], xs[...], NT, preferred_element_type=f32
-            )
-            return carry
-
-        lax.fori_loop(0, 2, one, 0)
+        base = pl.multiple_of(step * STEP, STEP)
+        acc[...] = lax.dot_general(
+            amat[pl.ds(base, STEP), :], xs[...], NT, preferred_element_type=f32
+        )
 
     def z_copy(d, s, u):
         rows = pl.ds(u * TILE, TILE)
@@ -234,33 +219,35 @@
     def y_copy(d, s):
         return remote(ys.at[d, s], yr.at[d, s], y_sem, (d, s), y_peer(1 if d == 0 else NY - 1))
 
-    def z_add(d, s, u):
+    def z_sum(d, s, u):
         z_copy(d, s - 1, u).wait_recv()
         rows = slice(d * 256 + u * TILE, d * 256 + (u + 1) * TILE)
-        acc[rows] += zr[d, s - 1, u * TILE : (u + 1) * TILE].astype(f32)
+        return acc[rows] + zr[d, s - 1, u * TILE : (u + 1) * TILE].astype(f32)
+
+    def z_add(d, s, u):
+        acc[d * 256 + u * TILE : d * 256 + (u + 1) * TILE] = z_sum(d, s, u)
+
+    def z_send(d, s, u, value):
+        zs[d, lax.rem(s, 2), u * TILE : (u + 1) * TILE] = value.astype(bf16)
+        z_copy(d, s, u).start()
 
     def z_part(d, s, u):
-        @pl.when(s > 0)
-        def _():
-            z_add(d, s, u)
+        value = z_sum(d, s, u)
 
         @pl.when(s > 1)
         def _():
             z_copy(d, s - 2, u).wait_send()
 
-        rows = slice(d * 256 + u * TILE, d * 256 + (u + 1) * TILE)
-        zs[d, lax.rem(s, 2), u * TILE : (u + 1) * TILE] = acc[rows].astype(bf16)
-        z_copy(d, s, u).start()
+        z_send(d, s, u, value)
+
+    def y_first(d, s):
+        ys[d, s] = acc[512 + d * 256 : 768 + d * 256].astype(bf16)
+        y_copy(d, s).start()
 
     def y_part(d, s):
-        rows = slice(512 + d * 256, 768 + d * 256)
-
-        @pl.when(s > 1)
-        def _():
-            y_copy(d, s - 2).wait_recv()
-            acc[rows] += yr[d, s - 2].astype(f32)
-
-        ys[d, s] = acc[rows].astype(bf16)
+        y_copy(d, s - 2).wait_recv()
+        value = acc[512 + d * 256 : 768 + d * 256] + yr[d, s - 2].astype(f32)
+        ys[d, s] = value.astype(bf16)
         y_copy(d, s).start()
 
     def y_last(part):
@@ -289,50 +276,93 @@
             p2_copy(part, slot).start()
 
     def ring_step(s, carry):
+        @pl.when(s + AHEAD < NZ + 1)
+        def _():
+            build_z(s + AHEAD - 1)
+
+        @pl.when(s + AHEAD < NZ)
+        def _():
+            build_y(s + AHEAD)
+
         product(s)
-
-        @pl.when(s + AHEAD < NZ)
-        def _():
-            build_z(s + AHEAD)
-
-        @pl.when(s + AHEAD + 1 < NZ)
-        def _():
-            build_y(s + AHEAD + 1)
-
         for d in range(2):
             z_part(d, s, 0)
 
-        @pl.when(s < 6)
+        @pl.when(s == 1)
+        def _():
+            for d in range(2):
+                y_first(d, s)
+
+        @pl.when(jnp.logical_and(s > 1, s < 6))
         def _():
             for d in range(2):
                 y_part(d, s)
 
         for d in range(2):
             z_part(d, s, 1)
+
+        @pl.when(s > 4)
+        def _():
+            def one(i, carry):
+                target_step(i)
+                return carry
+
+            lax.fori_loop(4 * s - 20, 4 * s - 16, one, 0)
+
         return carry
 
-    lax.fori_loop(0, NZ - 1, ring_step, 0)
+    product(0)
+    for u in range(2):
+        for d in range(2):
+            z_send(d, 0, u, acc[d * 256 + u * TILE : d * 256 + (u + 1) * TILE])
+            if u == 0:
+                y_first(d, 0)
+    lax.fori_loop(1, NZ - 1, ring_step, 0)
+    for copy in c_copies:
+        copy.start()
     y_last(0)
     p2_hop(0, 0)
     product(NZ - 1)
     p2_hop(0, 1)
     y_last(1)
     p2_hop(1, 0)
+    for copy in c_copies:
+        copy.wait()
+    mid = cin[z]
+    for k in range(1, NZ):
+        mid = mid + cin_in[k - 1]
+    cmid[...] = mid
+    for copy in m_copies:
+        copy.start()
+    for d in range(2):
+        z_add(d, NZ - 1, 0)
     p2_hop(0, 2)
-    p1_copies = [
-        remote(p1.at[lax.rem(y + k, NY)], p1_in.at[k - 1], p1_sem, (k - 1,), y_peer(k))
-        for k in range(1, NY)
-    ]
-    for u in range(2):
+    p2_hop(1, 1)
+    for d in range(2):
+        z_add(d, NZ - 1, 1)
+
+    def p1_copy(d, piece):
+        return remote(
+            p1.at[d, piece], p1_in.at[d, piece], p1_sem, (d, piece), y_peer(1 if d == 0 else NY - 1)
+        )
+
+    def p1_send(d, piece):
+        yi = lax.rem(y + (2 if piece == 0 else 1 if d == 0 else 3), NY)
+        half = d if piece in (0, 2) else 1 - d
+        value = acc[pl.ds(pl.multiple_of(yi * TILE + half * HALF, HALF), HALF), :]
+        if piece == 2:
+            p1_copy(d, 0).wait_recv()
+            value = value + p1_in[d, 0].astype(f32)
+        p1[d, piece] = value.astype(bf16)
+        p1_copy(d, piece).start()
+
+    for piece in range(2):
         for d in range(2):
-            z_add(d, NZ - 1, u)
-            first = (2 * d + u) * TILE
-            p1[2 * d + u] = acc[first : first + TILE].astype(bf16)
-    for copy in p1_copies:
-        copy.start()
-    p2_hop(1, 1)
+            p1_send(d, piece)
     p2_hop(0, 3)
     p2_hop(1, 2)
+    for d in range(2):
+        p1_send(d, 2)
     p2_hop(1, 3)
 
     for copy in m_copies:
@@ -347,11 +377,12 @@
         result = jnp.dot(normed, weight[...], preferred_element_type=f32) + bias[...]
         out[half * TILE : (half + 1) * TILE, :] = jnp.maximum(result, 0.0).astype(bf16)
 
-    for copy in p1_copies:
-        copy.wait()
     total = acc[pl.ds(pl.multiple_of(y * TILE, TILE), TILE), :]
-    for k in range(1, NY):
-        total = total + p1_in[k - 1].astype(f32)
+    for d in range(2):
+        for piece in (1, 2):
+            p1_copy(d, piece).wait_recv()
+        order = (2, 1) if d == 0 else (1, 2)
+        total = total + jnp.concatenate([p1_in[d, piece] for piece in order], axis=0).astype(f32)
     finish(0, total)
     totals = []
     for part in range(2):
@@ -376,6 +407,9 @@
     for part in range(2):
         for slot in range(7):
             p2_copy(part, slot).wait_send()
+    for d in range(2):
+        for piece in range(3):
+            p1_copy(d, piece).wait_send()
 
 
 def body(features, weight, bias, edge_src, edge_dst, tile_count):
@@ -391,8 +425,8 @@
         scratch_shapes=[
             pltpu.VMEM((NROW, units, SRC), bf16),
             pltpu.VMEM((F, SRC), bf16),
-            pltpu.VMEM((16, 128), f32),
-            pltpu.VMEM((NROW - 1, 16, 128), f32),
+            pltpu.VMEM((32, 64), f32),
+            pltpu.VMEM((NROW - 1, 32, 64), f32),
             pltpu.VMEM((NZ, 8, 128), f32),
             pltpu.VMEM((NZ - 1, 8, 128), f32),
             pltpu.VMEM((8, 128), f32),
@@ -402,8 +436,8 @@
             pltpu.VMEM((2, NZ - 1, 2 * TILE, F), bf16),
             pltpu.VMEM((2, 6, 2 * TILE, F), bf16),
             pltpu.VMEM((2, 6, 2 * TILE, F), bf16),
-            pltpu.VMEM((NY, TILE, F), bf16),
-            pltpu.VMEM((NY - 1, TILE, F), bf16),
+            pltpu.VMEM((2, 3, HALF, F), bf16),
+            pltpu.VMEM((2, 3, HALF, F), bf16),
             pltpu.VMEM((2, NZ, HALF, F), f32),
             pltpu.VMEM((2, 7, HALF, F), bf16),
             pltpu.VMEM((2, 7, HALF, F), bf16),
@@ -414,7 +448,7 @@
             dma((2, NY - 1)),
             dma((2, 2, NZ - 1, 2)),
             dma((2, 2, 6)),
-            dma((2, NY - 1)),
+            dma((2, 2, 3)),
             dma((2, 2, 7)),
             dma,
         ],

time: 91.3 us -> 91.8 us (level)
  no operation moved by 1% of the time
where the time goes in v3:
time: 91.8 us; the launch traced here: 91.7 us
  Pallas kernels  90 us (98%)
  local copies, waits for them, and re-layouts  1.67 us (2%)
    pallas_call x1, Pallas kernels, body(): pl.pallas_call(kernel, out_shape=jax.ShapeDtypeStruct((2 * TILE, F), bf16...  90 us

profile of v3, /device:TPU:8, one launch (start us, length us, event | category | flops | bytes accessed | tf_op | source)
XLA Modules:
  0.0 91.7 jit_solution(11394173258655501563)
XLA Ops:
  0.0 90.0 %graph_layer.1 = bf16[256,512]{1,0:T(8,128)(2,1)} custom-call(bf16[64,2048]{1,0:T(8,128)(2,1)} %bitcast.3, s32[64,512]{1,0:T(8,128)} %src.1, s32[64,512]{1,0:T(8,128)} %dst.1, s32[1,64]{1,0:T(1,128)} %bitcast.5, bf16[512,512]{1,0:T(8,128)(2,1)} %weight.1, f32[1,512]{1,0:T(1,128)} %bitcast.4), custom_call_target="tpu_custom_call" | custom-call | tf_op jit(solution)/shard_map/graph_layer/pallas_call | solution.py:420
  90.0 1.7 %copy.8 = bf16[256,512]{1,0:T(8,128)(2,1)} copy(bf16[256,512]{1,0:T(8,128)(2,1)} %graph_layer.1) | data formatting | bytes 524288

commit v4 on v3

--- a/solution.py
+++ b/solution.py
@@ -38,7 +38,7 @@
 def kernel(
     xt, src, dst, cnt, weight, bias, out,
     xg, xs, deg, deg_in, cin, cin_in, cmid, cmid_in, amat,
-    zs, zr, ys, yr, p1, p1_in, p2, p2_out, p2_in, acc,
+    zs, zr, ys, yr, p1, p1_in, p2, p2_out, p2_in, acc, acc_y,
     x_sem, d_sem, c_sem, m_sem, z_sem, y_sem, p1_sem, p2_sem, own_sem,
 ):
     r = lax.axis_index("row")
@@ -86,7 +86,7 @@
     before_across = x_copy(7, xg.at[before], xg.at[before], sibling)
     after_across = x_copy(8, xg.at[after], xg.at[after], sibling)
     opposite_across = x_copy(9, xg.at[opposite], xg.at[opposite], sibling)
-    for copy in (right_low, left_high, right_high, left_low, own_across):
+    for copy in (right_low, left_high, own_across):
         copy.start()
     own = pltpu.make_async_copy(xt, xg.at[r], own_sem)
     own.start()
@@ -111,6 +111,8 @@
     on_right.start()
     left_high.wait_recv()
     on_left.start()
+    right_high.start()
+    left_low.start()
 
     def target_step(zi):
         rows = []
@@ -121,6 +123,13 @@
                 lax.dot_general(jnp.ones((32, CAP), f8), right, NT, preferred_element_type=f32)[:1]
             )
         cin[zi] = jnp.concatenate(rows, axis=0)
+
+    def target_steps(first):
+        def one(i, carry):
+            target_step(i)
+            return carry
+
+        lax.fori_loop(first, first + 4, one, 0)
 
     c_copies = [
         remote(cin.at[lax.rem(z + k, NZ)], cin_in.at[k - 1], c_sem, (k - 1,), z_peer(k))
@@ -175,6 +184,7 @@
 
     build_y(0)
     lax.fori_loop(0, AHEAD, ahead, 0)
+    target_steps(0)
     for copy in d_copies:
         copy.wait()
     total = deg[...]
@@ -203,10 +213,10 @@
         copy.wait_recv()
     scale_rows(r + 1)
 
-    def product(step):
-        base = pl.multiple_of(step * STEP, STEP)
-        acc[...] = lax.dot_general(
-            amat[pl.ds(base, STEP), :], xs[...], NT, preferred_element_type=f32
+    def product(first, rows, target):
+        base = pl.multiple_of(first, 512)
+        target[:rows, :] = lax.dot_general(
+            amat[pl.ds(base, rows), :], xs[...], NT, preferred_element_type=f32
         )
 
     def z_copy(d, s, u):
@@ -234,9 +244,13 @@
     def z_part(d, s, u):
         value = z_sum(d, s, u)
 
-        @pl.when(s > 1)
-        def _():
+        if isinstance(s, int):
             z_copy(d, s - 2, u).wait_send()
+        else:
+
+            @pl.when(s > 1)
+            def _():
+                z_copy(d, s - 2, u).wait_send()
 
         z_send(d, s, u, value)
 
@@ -250,12 +264,12 @@
         ys[d, s] = value.astype(bf16)
         y_copy(d, s).start()
 
-    def y_last(part):
+    def y_last(part, source, offset):
         for d in range(2):
             y_copy(d, 4 + part).wait_recv()
             for u in range(4):
-                first = 512 + d * 256 + u * HALF
-                p2[part, 4 * d + u] = acc[first : first + HALF] + yr[
+                first = offset + d * 256 + u * HALF
+                p2[part, 4 * d + u] = source[first : first + HALF] + yr[
                     d, 4 + part, u * HALF : (u + 1) * HALF
                 ].astype(f32)
 
@@ -284,7 +298,7 @@
         def _():
             build_y(s + AHEAD)
 
-        product(s)
+        product(s * STEP, STEP, acc)
         for d in range(2):
             z_part(d, s, 0)
 
@@ -293,39 +307,37 @@
             for d in range(2):
                 y_first(d, s)
 
-        @pl.when(jnp.logical_and(s > 1, s < 6))
+        @pl.when(s > 1)
         def _():
             for d in range(2):
                 y_part(d, s)
 
         for d in range(2):
             z_part(d, s, 1)
-
-        @pl.when(s > 4)
-        def _():
-            def one(i, carry):
-                target_step(i)
-                return carry
-
-            lax.fori_loop(4 * s - 20, 4 * s - 16, one, 0)
-
         return carry
 
-    product(0)
+    product(0, STEP, acc)
     for u in range(2):
         for d in range(2):
             z_send(d, 0, u, acc[d * 256 + u * TILE : d * 256 + (u + 1) * TILE])
             if u == 0:
                 y_first(d, 0)
-    lax.fori_loop(1, NZ - 1, ring_step, 0)
+    lax.fori_loop(1, NZ - 2, ring_step, 0)
+    target_steps(4)
     for copy in c_copies:
         copy.start()
-    y_last(0)
+    product((NZ - 2) * STEP, STEP, acc)
+    for d in range(2):
+        z_part(d, NZ - 2, 0)
+    y_last(0, acc, 512)
     p2_hop(0, 0)
-    product(NZ - 1)
+    for d in range(2):
+        z_part(d, NZ - 2, 1)
+    product((NZ - 1) * STEP + 512, 512, acc_y)
     p2_hop(0, 1)
-    y_last(1)
+    y_last(1, acc_y, 0)
     p2_hop(1, 0)
+    product((NZ - 1) * STEP, 512, acc)
     for copy in c_copies:
         copy.wait()
     mid = cin[z]
@@ -442,6 +454,7 @@
             pltpu.VMEM((2, 7, HALF, F), bf16),
             pltpu.VMEM((2, 7, HALF, F), bf16),
             pltpu.VMEM((STEP, F), f32),
+            pltpu.VMEM((STEP // 2, F), f32),
             dma((2, 10)),
             dma((2, NROW - 1)),
             dma((2, NZ - 1)),

time: 91.8 us -> 92.4 us (level)
  no operation moved by 1% of the time
where the time goes in v4:
time: 92.4 us; the launch traced here: 92.3 us
  Pallas kernels  90.6 us (98%)
  local copies, waits for them, and re-layouts  1.67 us (2%)
    pallas_call x1, Pallas kernels, body(): pl.pallas_call(kernel, out_shape=jax.ShapeDtypeStruct((2 * TILE, F), bf16...  90.6 us

profile of v4, /device:TPU:8, one launch (start us, length us, event | category | flops | bytes accessed | tf_op | source)
XLA Modules:
  0.0 92.3 jit_solution(5241488728502250253)
XLA Ops:
  0.0 90.6 %graph_layer.1 = bf16[256,512]{1,0:T(8,128)(2,1)} custom-call(bf16[64,2048]{1,0:T(8,128)(2,1)} %bitcast.3, s32[64,512]{1,0:T(8,128)} %src.1, s32[64,512]{1,0:T(8,128)} %dst.1, s32[1,64]{1,0:T(1,128)} %bitcast.5, bf16[512,512]{1,0:T(8,128)(2,1)} %weight.1, f32[1,512]{1,0:T(1,128)} %bitcast.4), custom_call_target="tpu_custom_call" | custom-call | tf_op jit(solution)/shard_map/graph_layer/pallas_call | solution.py:432
  90.6 1.7 %copy.8 = bf16[256,512]{1,0:T(8,128)(2,1)} copy(bf16[256,512]{1,0:T(8,128)(2,1)} %graph_layer.1) | data formatting | bytes 524288

commit v5 on v4

--- a/solution.py
+++ b/solution.py
@@ -16,7 +16,7 @@
 NY = 4
 NZ = 8
 HALF = 64
-AHEAD = 3
+AHEAD = 2
 STEP = 1024
 bf16 = jnp.bfloat16
 f32 = jnp.float32
@@ -143,47 +143,44 @@
             onehot(place, 512), onehot(s & 511, 512), NT, preferred_element_type=f32
         ).astype(bf16)
 
-    def build_z(step):
-        for jj in range(4):
-            zi = lax.rem(z + NZ - 1 - step, NZ) if jj < 2 else lax.rem(z + 1 + step, NZ)
-            count = count_matrix(2 * (jj * NZ + zi))
-            base = pl.multiple_of(step * STEP + jj * TILE, TILE)
-            for h in range(4):
-                amat[pl.ds(base, TILE), h * 512 : (h + 1) * 512] = count[h * TILE : (h + 1) * TILE]
-
-    def build_y(group):
+    def build(p):
+        group = p // 2
+        is_y = lax.rem(p, 2)
         q = group // 2
         d = lax.rem(group, 2)
         yi = lax.rem(y + 2 * NY + (2 * d - 1) * (q + 1), NY)
         for jj in range(4):
-            count = count_matrix(2 * (yi * NZ + 4 * d + jj) + 1)
+            zi = lax.rem(z + NZ - 1 - group, NZ) if jj < 2 else lax.rem(z + 1 + group, NZ)
+            z_tile = 2 * (jj * NZ + zi)
+            y_tile = 2 * (yi * NZ + 4 * d + jj) + 1
+            count = count_matrix(z_tile + is_y * (y_tile - z_tile))
+            z_base = group * STEP + jj * TILE
+            y_base = 2 * q * STEP + 512 + d * 256 + jj * HALF
+            base = z_base + is_y * (y_base - z_base)
             for part in range(2):
-                base = pl.multiple_of((2 * q + part) * STEP + 512 + d * 256 + jj * HALF, HALF)
+                first = pl.multiple_of(base + part * (HALF + is_y * (STEP - HALF)), HALF)
                 for h in range(4):
                     start = h * TILE + part * HALF
-                    amat[pl.ds(base, HALF), h * 512 : (h + 1) * 512] = count[start : start + HALF]
-
-    def ahead(step, carry):
-        @pl.when(step == 0)
+                    amat[pl.ds(first, HALF), h * 512 : (h + 1) * 512] = count[start : start + HALF]
+
+    def ahead(p, carry):
+        @pl.when(p == 2)
         def _():
             right_high.wait_recv()
             before_across.start()
             left_low.wait_recv()
             after_across.start()
 
-        build_z(step)
-        build_y(step + 1)
-
-        @pl.when(step == 0)
+        @pl.when(p == 3)
         def _():
             on_right.wait_recv()
             on_left.wait_recv()
             opposite_across.start()
 
+        build(p)
         return carry
 
-    build_y(0)
-    lax.fori_loop(0, AHEAD, ahead, 0)
+    lax.fori_loop(0, 2 * AHEAD + 2, ahead, 0)
     target_steps(0)
     for copy in d_copies:
         copy.wait()
@@ -214,10 +211,14 @@
     scale_rows(r + 1)
 
     def product(first, rows, target):
-        base = pl.multiple_of(first, 512)
-        target[:rows, :] = lax.dot_general(
-            amat[pl.ds(base, rows), :], xs[...], NT, preferred_element_type=f32
-        )
+        def one(i, carry):
+            base = pl.multiple_of(first + i * 512, 512)
+            target[pl.ds(pl.multiple_of(i * 512, 512), 512), :] = lax.dot_general(
+                amat[pl.ds(base, 512), :], xs[...], NT, preferred_element_type=f32
+            )
+            return carry
+
+        lax.fori_loop(0, rows // 512, one, 0)
 
     def z_copy(d, s, u):
         rows = pl.ds(u * TILE, TILE)
@@ -244,13 +245,9 @@
     def z_part(d, s, u):
         value = z_sum(d, s, u)
 
-        if isinstance(s, int):
+        @pl.when(s > 1)
+        def _():
             z_copy(d, s - 2, u).wait_send()
-        else:
-
-            @pl.when(s > 1)
-            def _():
-                z_copy(d, s - 2, u).wait_send()
 
         z_send(d, s, u, value)
 
@@ -290,53 +287,62 @@
             p2_copy(part, slot).start()
 
     def ring_step(s, carry):
-        @pl.when(s + AHEAD < NZ + 1)
-        def _():
-            build_z(s + AHEAD - 1)
-
-        @pl.when(s + AHEAD < NZ)
-        def _():
-            build_y(s + AHEAD)
+        sends = s > 0
+
+        @pl.when(jnp.logical_and(s > 0, s < NZ - AHEAD))
+        def _():
+            def one(p, carry):
+                build(p)
+                return carry
+
+            lax.fori_loop(2 * (s + AHEAD), 2 * (s + AHEAD) + 2, one, 0)
+
+        @pl.when(s == NZ - 2)
+        def _():
+            target_steps(4)
+            for copy in c_copies:
+                copy.start()
 
         product(s * STEP, STEP, acc)
-        for d in range(2):
-            z_part(d, s, 0)
-
-        @pl.when(s == 1)
+
+        @pl.when(s == 0)
+        def _():
+            for u in range(2):
+                for d in range(2):
+                    z_send(d, s, u, acc[d * 256 + u * TILE : d * 256 + (u + 1) * TILE])
+
+        @pl.when(sends)
+        def _():
+            for d in range(2):
+                z_part(d, s, 0)
+
+        @pl.when(s < 2)
         def _():
             for d in range(2):
                 y_first(d, s)
 
-        @pl.when(s > 1)
+        @pl.when(jnp.logical_and(s > 1, s < 6))
         def _():
             for d in range(2):
                 y_part(d, s)
 
-        for d in range(2):
-            z_part(d, s, 1)
+        @pl.when(s == 6)
+        def _():
+            y_last(0, acc, 512)
+            p2_hop(0, 0)
+            product((NZ - 1) * STEP + 512, 512, acc_y)
+
+        @pl.when(sends)
+        def _():
+            for d in range(2):
+                z_part(d, s, 1)
+
         return carry
 
-    product(0, STEP, acc)
-    for u in range(2):
-        for d in range(2):
-            z_send(d, 0, u, acc[d * 256 + u * TILE : d * 256 + (u + 1) * TILE])
-            if u == 0:
-                y_first(d, 0)
-    lax.fori_loop(1, NZ - 2, ring_step, 0)
-    target_steps(4)
-    for copy in c_copies:
-        copy.start()
-    product((NZ - 2) * STEP, STEP, acc)
-    for d in range(2):
-        z_part(d, NZ - 2, 0)
-    y_last(0, acc, 512)
-    p2_hop(0, 0)
-    for d in range(2):
-        z_part(d, NZ - 2, 1)
-    product((NZ - 1) * STEP + 512, 512, acc_y)
-    p2_hop(0, 1)
+    lax.fori_loop(0, NZ - 1, ring_step, 0)
     y_last(1, acc_y, 0)
     p2_hop(1, 0)
+    p2_hop(0, 1)
     product((NZ - 1) * STEP, 512, acc)
     for copy in c_copies:
         copy.wait()
@@ -384,10 +390,12 @@
         degree = degree + cmid_in[k - 1, pl.ds(2 * y, 2), :]
     norm = jnp.transpose(lax.rsqrt(1.0 + jnp.concatenate([degree] * 4, axis=0)))
 
-    def finish(half, total):
-        normed = (total * norm[:, half : half + 1]).astype(bf16)
+    def finish(first, total):
+        rows = total.shape[0]
+        half, start = first // TILE, first % TILE
+        normed = (total * norm[start : start + rows, half : half + 1]).astype(bf16)
         result = jnp.dot(normed, weight[...], preferred_element_type=f32) + bias[...]
-        out[half * TILE : (half + 1) * TILE, :] = jnp.maximum(result, 0.0).astype(bf16)
+        out[first : first + rows, :] = jnp.maximum(result, 0.0).astype(bf16)
 
     total = acc[pl.ds(pl.multiple_of(y * TILE, TILE), TILE), :]
     for d in range(2):
@@ -396,14 +404,12 @@
         order = (2, 1) if d == 0 else (1, 2)
         total = total + jnp.concatenate([p1_in[d, piece] for piece in order], axis=0).astype(f32)
     finish(0, total)
-    totals = []
     for part in range(2):
         total = p2[part, z]
         for slot in (3, 6):
             p2_copy(part, slot).wait_recv()
             total = total + p2_in[part, slot].astype(f32)
-        totals.append(total)
-    finish(1, jnp.concatenate(totals, axis=0))
+        finish(TILE + part * HALF, total)
 
     for copy in (
         right_low, left_high, right_high, left_low, own_across,

time: 92.4 us -> 91.2 us (0.987)
  Pallas kernels: 90.6 us -> 89.3 us
    pallas_call x1, Pallas kernels: 90.6 us -> 89.3 us  [body(): pl.pallas_call(kernel, out_shape=jax.ShapeDtypeStruct((2 * TILE, F), bf16...]
where the time goes in v5:
time: 91.2 us; the launch traced here: 91 us
  Pallas kernels  89.3 us (98%)
  local copies, waits for them, and re-layouts  1.67 us (2%)
    pallas_call x1, Pallas kernels, body(): pl.pallas_call(kernel, out_shape=jax.ShapeDtypeStruct((2 * TILE, F), bf16...  89.3 us

profile of v5, /device:TPU:8, one launch (start us, length us, event | category | flops | bytes accessed | tf_op | source)
XLA Modules:
  0.0 91.0 jit_solution(15467187172420690363)
XLA Ops:
  0.0 89.3 %graph_layer.1 = bf16[256,512]{1,0:T(8,128)(2,1)} custom-call(bf16[64,2048]{1,0:T(8,128)(2,1)} %bitcast.3, s32[64,512]{1,0:T(8,128)} %src.1, s32[64,512]{1,0:T(8,128)} %dst.1, s32[1,64]{1,0:T(1,128)} %bitcast.5, bf16[512,512]{1,0:T(8,128)(2,1)} %weight.1, f32[1,512]{1,0:T(1,128)} %bitcast.4), custom_call_target="tpu_custom_call" | custom-call | tf_op jit(solution)/shard_map/graph_layer/pallas_call | solution.py:438
  89.3 1.7 %copy.8 = bf16[256,512]{1,0:T(8,128)(2,1)} copy(bf16[256,512]{1,0:T(8,128)(2,1)} %graph_layer.1) | data formatting | bytes 524288

commit v6 on v5

--- a/solution.py
+++ b/solution.py
@@ -297,45 +297,56 @@
 
             lax.fori_loop(2 * (s + AHEAD), 2 * (s + AHEAD) + 2, one, 0)
 
-        @pl.when(s == NZ - 2)
+        product(s * STEP, STEP, acc)
+
+        @pl.when(s == 0)
+        def _():
+            for u in range(2):
+                for d in range(2):
+                    z_send(d, s, u, acc[d * 256 + u * TILE : d * 256 + (u + 1) * TILE])
+
+        @pl.when(sends)
+        def _():
+            for d in range(2):
+                z_part(d, s, 0)
+
+        @pl.when(s < 2)
+        def _():
+            for d in range(2):
+                y_first(d, s)
+
+        @pl.when(jnp.logical_and(s > 1, s < 6))
+        def _():
+            for d in range(2):
+                y_part(d, s)
+
+        @pl.when(s == 6)
+        def _():
+            y_last(0, acc, 512)
+            p2_hop(0, 0)
+            product((NZ - 1) * STEP + 512, 512, acc_y)
+
+        @pl.when(sends)
+        def _():
+            for d in range(2):
+                z_part(d, s, 1)
+
+        @pl.when(s == 0)
         def _():
             target_steps(4)
             for copy in c_copies:
                 copy.start()
 
-        product(s * STEP, STEP, acc)
-
-        @pl.when(s == 0)
-        def _():
-            for u in range(2):
-                for d in range(2):
-                    z_send(d, s, u, acc[d * 256 + u * TILE : d * 256 + (u + 1) * TILE])
-
-        @pl.when(sends)
-        def _():
-            for d in range(2):
-                z_part(d, s, 0)
-
-        @pl.when(s < 2)
-        def _():
-            for d in range(2):
-                y_first(d, s)
-
-        @pl.when(jnp.logical_and(s > 1, s < 6))
-        def _():
-            for d in range(2):
-                y_part(d, s)
-
-        @pl.when(s == 6)
-        def _():
-            y_last(0, acc, 512)
-            p2_hop(0, 0)
-            product((NZ - 1) * STEP + 512, 512, acc_y)
-
-        @pl.when(sends)
-        def _():
-            for d in range(2):
-                z_part(d, s, 1)
+        @pl.when(s == 3)
+        def _():
+            for copy in c_copies:
+                copy.wait()
+            mid = cin[z]
+            for k in range(1, NZ):
+                mid = mid + cin_in[k - 1]
+            cmid[...] = mid
+            for copy in m_copies:
+                copy.start()
 
         return carry
 
@@ -344,14 +355,6 @@
     p2_hop(1, 0)
     p2_hop(0, 1)
     product((NZ - 1) * STEP, 512, acc)
-    for copy in c_copies:
-        copy.wait()
-    mid = cin[z]
-    for k in range(1, NZ):
-        mid = mid + cin_in[k - 1]
-    cmid[...] = mid
-    for copy in m_copies:
-        copy.start()
     for d in range(2):
         z_add(d, NZ - 1, 0)
     p2_hop(0, 2)
@@ -381,14 +384,25 @@
     p2_hop(1, 2)
     for d in range(2):
         p1_send(d, 2)
-    p2_hop(1, 3)
-
+    for copy in (
+        right_low, left_high, right_high, left_low, own_across,
+        on_right, on_left, before_across, after_across, opposite_across,
+    ):
+        copy.wait_send()
+    for d in range(2):
+        for s in (NZ - 3, NZ - 2):
+            for u in range(2):
+                z_copy(d, s, u).wait_send()
+        for s in range(6):
+            y_copy(d, s).wait_send()
     for copy in m_copies:
         copy.wait()
     degree = cmid[pl.ds(2 * y, 2), :]
     for k in range(1, NY):
         degree = degree + cmid_in[k - 1, pl.ds(2 * y, 2), :]
     norm = jnp.transpose(lax.rsqrt(1.0 + jnp.concatenate([degree] * 4, axis=0)))
+
+    p2_hop(1, 3)
 
     def finish(first, total):
         rows = total.shape[0]
@@ -411,17 +425,6 @@
             total = total + p2_in[part, slot].astype(f32)
         finish(TILE + part * HALF, total)
 
-    for copy in (
-        right_low, left_high, right_high, left_low, own_across,
-        on_right, on_left, before_across, after_across, opposite_across,
-    ):
-        copy.wait_send()
-    for d in range(2):
-        for s in (NZ - 3, NZ - 2):
-            for u in range(2):
-                z_copy(d, s, u).wait_send()
-        for s in range(6):
-            y_copy(d, s).wait_send()
     for part in range(2):
         for slot in range(7):
             p2_copy(part, slot).wait_send()

time: 91.2 us -> 91.4 us (level)
  no operation moved by 1% of the time
where the time goes in v6:
time: 91.4 us; the launch traced here: 91.2 us
  Pallas kernels  89.6 us (98%)
  local copies, waits for them, and re-layouts  1.67 us (2%)
    pallas_call x1, Pallas kernels, body(): pl.pallas_call(kernel, out_shape=jax.ShapeDtypeStruct((2 * TILE, F), bf16...  89.6 us

profile of v6, /device:TPU:8, one launch (start us, length us, event | category | flops | bytes accessed | tf_op | source)
XLA Modules:
  0.0 91.2 jit_solution(9744105594536297139)
XLA Ops:
  0.0 89.6 %graph_layer.1 = bf16[256,512]{1,0:T(8,128)(2,1)} custom-call(bf16[64,2048]{1,0:T(8,128)(2,1)} %bitcast.3, s32[64,512]{1,0:T(8,128)} %src.1, s32[64,512]{1,0:T(8,128)} %dst.1, s32[1,64]{1,0:T(1,128)} %bitcast.5, bf16[512,512]{1,0:T(8,128)(2,1)} %weight.1, f32[1,512]{1,0:T(1,128)} %bitcast.4), custom_call_target="tpu_custom_call" | custom-call | tf_op jit(solution)/shard_map/graph_layer/pallas_call | solution.py:441
  89.6 1.7 %copy.8 = bf16[256,512]{1,0:T(8,128)(2,1)} copy(bf16[256,512]{1,0:T(8,128)(2,1)} %graph_layer.1) | data formatting | bytes 524288

commit v7 on v5

--- a/solution.py
+++ b/solution.py
@@ -305,6 +305,16 @@
 
         product(s * STEP, STEP, acc)
 
+        @pl.when(s < 2)
+        def _():
+            for d in range(2):
+                y_first(d, s)
+
+        @pl.when(jnp.logical_and(s > 1, s < 6))
+        def _():
+            for d in range(2):
+                y_part(d, s)
+
         @pl.when(s == 0)
         def _():
             for u in range(2):
@@ -315,16 +325,6 @@
         def _():
             for d in range(2):
                 z_part(d, s, 0)
-
-        @pl.when(s < 2)
-        def _():
-            for d in range(2):
-                y_first(d, s)
-
-        @pl.when(jnp.logical_and(s > 1, s < 6))
-        def _():
-            for d in range(2):
-                y_part(d, s)
 
         @pl.when(s == 6)
         def _():

time: 91.2 us -> 91.6 us (level)
  no operation moved by 1% of the time
where the time goes in v7:
time: 91.6 us; the launch traced here: 91.4 us
  Pallas kernels  89.7 us (98%)
  local copies, waits for them, and re-layouts  1.67 us (2%)
    pallas_call x1, Pallas kernels, body(): pl.pallas_call(kernel, out_shape=jax.ShapeDtypeStruct((2 * TILE, F), bf16...  89.7 us

profile of v7, /device:TPU:8, one launch (start us, length us, event | category | flops | bytes accessed | tf_op | source)
XLA Modules:
  0.0 91.4 jit_solution(1093712601995545731)
XLA Ops:
  0.0 89.7 %graph_layer.1 = bf16[256,512]{1,0:T(8,128)(2,1)} custom-call(bf16[64,2048]{1,0:T(8,128)(2,1)} %bitcast.3, s32[64,512]{1,0:T(8,128)} %src.1, s32[64,512]{1,0:T(8,128)} %dst.1, s32[1,64]{1,0:T(1,128)} %bitcast.5, bf16[512,512]{1,0:T(8,128)(2,1)} %weight.1, f32[1,512]{1,0:T(1,128)} %bitcast.4), custom_call_target="tpu_custom_call" | custom-call | tf_op jit(solution)/shard_map/graph_layer/pallas_call | solution.py:438
  89.7 1.7 %copy.8 = bf16[256,512]{1,0:T(8,128)(2,1)} copy(bf16[256,512]{1,0:T(8,128)(2,1)} %graph_layer.1) | data formatting | bytes 524288
